TPU v7x, 256 devices: a whole 4x4x8 slice. The times are simulated.
256 devices in a mesh: tp: 4 (over y), ep: 64 (over z, x, core).
Axes of the slice: x: 4, y: 4, z: 8, core: 2. Of those that a mesh axis runs over, the one named last changes fastest.
Arguments:
- grad_out: bfloat16 [8192, 5120], P('ep', 'tp'), may hold values from -1.5 to 1.5
- routes: int32 [8192, 6], P('ep'), may hold values from 0 to 63, all different within a row; in each aligned block of 128 rows (0 to 127, 128 to 255, ...) at most 24 rows name the same one
- gates: float32 [8192, 6], P('ep'), may hold values from 0.03 to 0.6
- saved_gate: bfloat16 [64, 64, 24, 1536], P('ep', None, None, 'tp'), may hold values from -6 to 6
- saved_up: bfloat16 [64, 64, 24, 1536], P('ep', None, None, 'tp'), may hold values from -6 to 6
- w_down: bfloat16 [64, 1536, 5120], P('ep', 'tp'), may hold values from -0.15625 to 0.15625
Outputs:
- grad_gate: bfloat16 [64, 64, 24, 1536], P('ep', None, None, 'tp')
- grad_up: bfloat16 [64, 64, 24, 1536], P('ep', None, None, 'tp')
- grad_w_down: bfloat16 [64, 1536, 5120], P('ep', 'tp')
- grad_gates: float32 [8192, 6], P('ep')
Inputs may be any that keep to these rules, and one draw needn't show every extreme that they name: `routes`: the 6 ids of a row differ. In each aligned block of 128 rows (the tokens of one index of ep) no id is named by more than 24 rows, and some id reaches 24 in some block; every id is named somewhere.
All inputs are finite; a program needn't handle non-finite values.
Results may differ from a plain program's by a relative error of at most 0.007.
Values may be sent and summed in bfloat16 or wider, within the bound.
A program may use at most 128 MiB of HBM per device.

v0:
```python
import jax
import jax.numpy as jnp
from jax import lax
from jax.sharding import PartitionSpec as P


def slot_numbers(routes, experts):
    flat_routes = routes.reshape(-1)
    onehot = (flat_routes[:, None] == jnp.arange(experts, dtype=jnp.int32)[None, :]).astype(
        jnp.int32
    )
    earlier = jnp.cumsum(onehot, axis=0) - onehot
    return jnp.sum(earlier * onehot, axis=1).reshape(routes.shape)


def body(grad_out, routes, gates, saved_gate, saved_up, w_down):
    experts = lax.axis_size("ep")
    capacity = saved_gate.shape[2]
    slot_ids = slot_numbers(routes, experts)
    target = routes * capacity + slot_ids
    places = jnp.arange(experts * capacity, dtype=jnp.int32)
    matches = target[None, :, :] == places[:, None, None]
    picker = jnp.any(matches, axis=2).astype(jnp.bfloat16)
    weights = jnp.sum(jnp.where(matches, gates[None, :, :], jnp.float32(0.0)), axis=(1, 2)).reshape(
        experts, capacity
    )
    gathered = lax.all_gather(grad_out, "tp", axis=1, tiled=True)
    packed = jnp.dot(picker, gathered, preferred_element_type=jnp.float32).astype(jnp.bfloat16)
    packed = packed.reshape(experts, capacity, gathered.shape[1])
    routed = lax.all_to_all(packed, "ep", split_axis=0, concat_axis=0, tiled=True)
    slot_prob = lax.all_to_all(weights, "ep", split_axis=0, concat_axis=0, tiled=True)
    slot_count = routed.shape[0] * routed.shape[1]
    flat_rows = routed.reshape(slot_count, routed.shape[2])
    flat_prob = slot_prob.reshape(slot_count, 1)
    gate_vals = saved_gate.reshape(slot_count, saved_gate.shape[3]).astype(jnp.float32)
    up_vals = saved_up.reshape(slot_count, saved_up.shape[3]).astype(jnp.float32)
    weight = w_down[0]
    grad_hidden = lax.dot_general(
        flat_rows, weight, (((1,), (1,)), ((), ())), preferred_element_type=jnp.float32
    )
    sigmoid = jax.nn.sigmoid(gate_vals)
    activation = gate_vals * sigmoid
    hidden = (activation * up_vals).astype(jnp.bfloat16)
    slot_grad = jnp.sum(hidden.astype(jnp.float32) * grad_hidden, axis=1)
    scaled_hidden = flat_prob * grad_hidden
    slope = sigmoid * (1.0 + gate_vals * (1.0 - sigmoid))
    grad_gate = (scaled_hidden * up_vals * slope).astype(jnp.bfloat16).reshape(saved_gate.shape)
    grad_up = (scaled_hidden * activation).astype(jnp.bfloat16).reshape(saved_up.shape)
    scaled = (flat_prob * flat_rows.astype(jnp.float32)).astype(jnp.bfloat16)
    grad_weight = lax.dot_general(
        hidden, scaled, (((0,), (0,)), ((), ())), preferred_element_type=jnp.float32
    )
    grad_w_down = grad_weight.astype(jnp.bfloat16)[None]
    returned = lax.all_to_all(
        slot_grad.reshape(routed.shape[0], routed.shape[1]),
        "ep",
        split_axis=0,
        concat_axis=0,
        tiled=True,
    )
    flat_back = returned.reshape(-1)
    picked = jnp.sum(jnp.where(matches, flat_back[:, None, None], jnp.float32(0.0)), axis=0)
    grad_gates = lax.psum(picked, "tp")
    return (grad_gate, grad_up, grad_w_down, grad_gates)


def solution(mesh):
    in_specs = (
        P("ep", "tp"),
        P("ep", None),
        P("ep", None),
        P("ep", None, None, "tp"),
        P("ep", None, None, "tp"),
        P("ep", "tp", None),
    )
    out_specs = (
        P("ep", None, None, "tp"),
        P("ep", None, None, "tp"),
        P("ep", "tp", None),
        P("ep", None),
    )
    return jax.shard_map(body, mesh=mesh, in_specs=in_specs, out_specs=out_specs, check_vma=False)
```

profile of v0, /device:TPU:1, one launch (start us, length us, event | category | flops | bytes accessed | tf_op | source)
XLA Modules:
  0.0 483.7 jit_solution(16646786929341067452)
XLA Ops:
  7.2 0.0 all-gather.2.cloned.1.call-start
  7.2 0.7 all-gather.2.cloned.1.call-update
  7.9 0.8 copy.34
  8.7 0.1 eq.42
  8.8 0.1 eq.38
  9.0 1.8 reduce-window.6
  10.8 0.3 slice_reduce_fusion
  11.1 0.1 fusion.19
  11.2 0.1 reshape.69
  11.4 0.1 copy.37
  11.4 0.7 multiply_add_fusion
  12.2 0.8 fusion.1
  13.0 27.0 %all-gather.2.cloned.1.call-done = bf16[128,5120]{1,0:T(8,128)(2,1)} async-done(((bf16[128,1280]{1,0:T(8,128)(2,1)}), bf16[128,5120]{1,0:T(8,128)(2,1)}) %all-gather.2.cloned.1.call-update) | async-done | bytes 1310736 | tf_op jit(solution)/shard_map/all_gather | solution.py:27
  40.0 9.0 %convolution_convert_fusion = bf16[1536,5120]{1,0:T(8,128)(2,1)} fusion(pred[1536,128]{1,0:T(8,128)(4,1)S(1)} %fusion.1, bf16[128,5120]{1,0:T(8,128)(2,1)} %all-gather.2.cloned.1.call-done), kind=kOutput, calls=%fused_computation.1 | convolution fusion | flops 2021130240 | bytes 17235968 | tf_op jit(solution)/shard_map/dot_general | solution.py:28
  49.0 354.4 %all_to_all.23 = bf16[64,24,5120]{2,1,0:T(8,128)(2,1)S(1)} all-to-all(bf16[64,24,5120]{2,1,0:T(8,128)(2,1)} %bitcast.76), channel_id=1, replica_groups=mesh['tp'=4,'ep'=64] {'ep'}, dimensions={0} | all-to-all | bytes 31457280 | tf_op jit(solution)/shard_map/all_to_all | solution.py:30
  403.4 14.9 %multiply_reduce_fusion = (f32[1536]{0:T(1024)S(1)}, f32[1536,384]{1,0:T(8,128)}) fusion(bf16[1,64,24,384]{3,2,1,0:T(8,128)(2,1)S(1)} %copy-done.1, bf16[1,64,24,384]{3,2,1,0:T(8,128)(2,1)S(1)} %copy-done.2, bf16[1536,5120]{1,0:T(8,128)(2,1)S(1)} %bitcast.77, bf16[1,384,5120]{2,1,0:T(8,128)(2,1)} %param.11), kind=kOutput, calls=%fused_computation.29 | convolution fusion | flops 6046284288 | bytes 24385536 | tf_op jit(solution)/shard_map/dot_general | solution.py:38
  418.3 0.1 all_to_all.18
  418.4 15.8 %all_to_all.24 = f32[64,1,24]{2,1,0:T(1,128)S(1)} all-to-all(f32[64,1,24]{2,1,0:T(1,128)S(1)} %bitcast.82), channel_id=1, replica_groups=mesh['tp'=4,'ep'=64] {'ep'}, dimensions={0} | all-to-all | bytes 12288 | tf_op jit(solution)/shard_map/all_to_all | solution.py:54
  434.2 0.5 broadcast.45
  434.7 0.7 reduce.9
  435.4 0.1 broadcast_in_dim.34
  435.5 1.4 select_reduce_fusion
  436.9 0.7 all_to_all.15
  437.6 5.4 %all-to-all-start = ((f32[64,1,24]{2,1,0:T(1,128)}), f32[64,1,24]{2,1,0:T(1,128)}, u32[]{:S(2)}, u32[]{:S(2)}) async-start(f32[64,1,24]{2,1,0:T(1,128)} %bitcast.1), calls=%async_computation | async-start | bytes 65536 | tf_op jit(solution)/shard_map/all_to_all | solution.py:31
  443.1 0.8 fusion.16
  443.8 8.8 %psum.7 = f32[128,6]{0,1:T(8,128)} all-reduce(f32[128,6]{0,1:T(8,128)S(1)} %get-tuple-element.4), channel_id=1, replica_groups=mesh['tp'=4,'ep'=64] {'tp'}, use_global_device_ids=true, to_apply=%region_7.8 | all-reduce | flops 768 | bytes 6144 | tf_op jit(solution)/shard_map/psum | solution.py:63
  452.6 0.0 all-to-all-done
  452.6 2.1 reduce.8
  454.7 0.8 mul.63
  455.5 4.0 multiply_convert_fusion.1
  459.5 9.1 %multiply_convert_fusion = bf16[64,24,5120]{2,1,0:T(8,128)(2,1)S(1)} fusion(bf16[64,24,5120]{2,1,0:T(8,128)(2,1)} %copy-done, f32[64,24]{1,0:T(8,128)} %bitcast.10), kind=kLoop, calls=%fused_computation | loop fusion | flops 23592960 | bytes 31463424 | tf_op jit(solution)/shard_map/convert_element_type | solution.py:49
  468.6 8.2 %fusion = bf16[1,384,5120]{2,1,0:T(8,128)(2,1)} fusion(bf16[1536,384]{1,0:T(8,128)(2,1)S(1)} %bitcast.79, bf16[1536,5120]{1,0:T(8,128)(2,1)S(1)} %bitcast.78), kind=kOutput, calls=%fused_computation.3 | convolution fusion | flops 6041763840 | bytes 20840448 | tf_op jit(solution)/shard_map/dot_general | solution.py:50
  (10 shorter events, 0.1 us)
Async XLA Ops:
  7.2 32.8 %all-gather.2.cloned.1.call-start = ((), (), s32[]{:S(2)}) async-start(), calls=%async_computation.3 | async-start | bytes 1638400 | tf_op jit(solution)/shard_map/all_gather | solution.py:27
  49.0 354.4 %copy-start.1 = (bf16[1,64,24,384]{3,2,1,0:T(8,128)(2,1)S(1)}, bf16[1,64,24,384]{3,2,1,0:T(8,128)(2,1)}, u32[]{:S(2)}) copy-start(bf16[1,64,24,384]{3,2,1,0:T(8,128)(2,1)} %param.10) | copy-start | bytes 3538948
  49.0 354.4 %copy-start.2 = (bf16[1,64,24,384]{3,2,1,0:T(8,128)(2,1)S(1)}, bf16[1,64,24,384]{3,2,1,0:T(8,128)(2,1)}, u32[]{:S(2)}) copy-start(bf16[1,64,24,384]{3,2,1,0:T(8,128)(2,1)} %param.9) | copy-start | bytes 3538948
  403.4 14.9 %copy-start = (bf16[64,24,5120]{2,1,0:T(8,128)(2,1)}, bf16[64,24,5120]{2,1,0:T(8,128)(2,1)S(1)}, u32[]{:S(2)}) copy-start(bf16[64,24,5120]{2,1,0:T(8,128)(2,1)S(1)} %all_to_all.23) | copy-start | bytes 47185924
  403.4 32.1 %copy-start.3 = (f32[128,6]{0,1:T(8,128)S(1)}, f32[128,6]{0,1:T(8,128)}, u32[]{:S(2)}) copy-start(f32[128,6]{0,1:T(8,128)} %param.8) | copy-start | bytes 9220
  437.6 15.0 %all-to-all-start = ((f32[64,1,24]{2,1,0:T(1,128)}), f32[64,1,24]{2,1,0:T(1,128)}, u32[]{:S(2)}, u32[]{:S(2)}) async-start(f32[64,1,24]{2,1,0:T(1,128)} %bitcast.1), calls=%async_computation | async-start | bytes 65536 | tf_op jit(solution)/shard_map/all_to_all | solution.py:31
Sparse Core Ops, SparseCore 0:
  9.8 30.1 all-gather.1
where the time goes:
time: 485 us; the launch traced here: 484 us
  blocking collectives  379 us (78%)
  matrix products  32.1 us (7%)
  waiting for transfers between devices  27.7 us (6%)
  other arithmetic  21.6 us (4%)
  between operations  14.1 us (3%)
  starting transfers between devices  5.47 us (1%)
    all_to_all x1, blocking collectives, body(): lax.all_to_all(packed, 'ep', split_axis=0, concat_axis=0, tiled=True)  354 us
    all_gather x1, waiting for transfers between devices, body(): gathered = lax.all_gather(grad_out, 'tp', axis=1, tiled=True)  27 us
    all_to_all x1, blocking collectives, body(): lax.all_to_all(slot_grad.reshape(routed.shape[0], routed.shape[1]), 'ep',...  15.8 us
    dot_general x1, matrix products, body(): lax.dot_general(flat_rows, weight, (((1,), (1,)), ((), ())), preferred_el...  14.9 us
  transfers between devices with their start and end apart: 2, of which 1 were waited for; matrix products, arithmetic and copies ran while one was open for 1% of the time, Pallas kernels for 0%

commit v1 on v0

v1 whole, which is shorter than its diff:
```python
import functools

import jax
import jax.numpy as jnp
from jax import lax
from jax.experimental import pallas as pl
from jax.experimental.pallas import tpu as pltpu
from jax.sharding import PartitionSpec as P

NZ, NX, NY = 8, 4, 4
CAP = 24
TOK = 128
TOP = 6
EXTRA = 256
META = 128
SLAB = 2 * CAP
ROWS = NX * SLAB
PARTNER_SLOT = (0, 2, 1, 4, 3, 6, 5, 7)
OFFSETS = (0, -1, 1, -2, 2, -3, 3, -4)
F32 = jnp.float32
BF16 = jnp.bfloat16
MESH = pl.DeviceIdType.MESH


def chunks(total, size):
    return [(at, min(size, total - at)) for at in range(0, total, size)]


def kernel(
    feats,
    width,
    tok_ref,
    meta_ref,
    gate_hbm,
    up_hbm,
    w_hbm,
    gg_ref,
    gu_ref,
    gw_ref,
    sl_ref,
    tok,
    pk,
    rx,
    ro,
    ry,
    w,
    sg,
    su,
    hs,
    hst,
    in_sem,
    e_send,
    e_recv,
    z_send,
    z_recv,
    c_send,
    c_recv,
    x_send,
    x_recv,
    y_send,
    y_recv,
):
    y = lax.axis_index("tp")
    ep = lax.axis_index("ep")
    z = ep // 8
    x = (ep // 2) % 4
    c = ep % 2
    d = 1 - 2 * c
    main = feats - EXTRA

    def ep_at(zz, xx, cc):
        return {"ep": zz * 8 + xx * 2 + cc}

    z_fwd, z_bwd = ep_at((z + d + 8) % 8, x, c), ep_at((z - d + 8) % 8, x, c)
    x_fwd, x_bwd = ep_at(z, (x + d + 4) % 4, c), ep_at(z, (x - d + 4) % 4, c)
    y_fwd, y_bwd = {"tp": (y + d + 4) % 4}, {"tp": (y - d + 4) % 4}
    partner = ep_at(z, x, 1 - c)

    barrier = pltpu.get_barrier_semaphore()
    for peer in (z_fwd, z_bwd, x_fwd, x_bwd, y_fwd, y_bwd, partner):
        pl.semaphore_signal(barrier, inc=1, device_id=peer, device_id_type=MESH)

    loads = [
        pltpu.make_async_copy(w_hbm, w, in_sem.at[0]),
        pltpu.make_async_copy(gate_hbm, sg, in_sem.at[1]),
        pltpu.make_async_copy(up_hbm, su, in_sem.at[2]),
    ]
    for load in loads:
        load.start()
    tok[0, 0:TOK, 0:feats] = tok_ref[...]
    tok[0, 0:TOK, width - META : width] = meta_ref[...]
    pl.semaphore_wait(barrier, 7)

    sends = []

    def remote(src, dst, send, recv, peer):
        return pltpu.make_async_remote_copy(
            src_ref=src,
            dst_ref=dst,
            send_sem=send,
            recv_sem=recv,
            device_id=peer,
            device_id_type=MESH,
        )

    def start(*args):
        copy = remote(*args)
        copy.start()
        sends.append(copy)

    def extra_at(slot):
        return tok.at[0, 0:TOK, pl.ds(pl.multiple_of(feats + slot * EXTRA, 128), EXTRA)]

    from_bwd, from_fwd = (3 - d) % 4, (3 + d) % 4
    mine = tok_ref.at[:, main:feats]
    start(mine, extra_at(from_bwd), e_send.at[0], e_recv.at[0], y_fwd)
    start(mine, extra_at(from_fwd), e_send.at[1], e_recv.at[1], y_bwd)
    remote(mine, extra_at(from_bwd), e_send.at[0], e_recv.at[0], y_bwd).wait_recv()
    start(extra_at(from_bwd), extra_at(1), e_send.at[2], e_recv.at[2], y_fwd)
    remote(mine, extra_at(from_fwd), e_send.at[1], e_recv.at[1], y_fwd).wait_recv()
    remote(mine, extra_at(1), e_send.at[2], e_recv.at[2], y_bwd).wait_recv()

    def own(j):
        return tok.at[j, 0:TOK]

    def other(j):
        return tok.at[j, TOK : 2 * TOK]

    def z_copy(src, dst, peer):
        return (own(src), own(dst), z_send.at[dst], z_recv.at[dst], peer)

    def row_ids(j, half, core):
        table = tok[j, half * TOK : (half + 1) * TOK, width - META : width].astype(F32).T
        expert = table[0:8].astype(jnp.int32) - 1
        slot = table[32:40].astype(jnp.int32)
        hit = (lax.shift_right_arithmetic(expert, 3) == z) & ((expert & 1) == c)
        relative = ((lax.shift_right_arithmetic(expert, 1) & 3) - x) * d & 3
        return jnp.where(hit, relative * SLAB + core * CAP + slot, -1)

    def one_hot(ids):
        rows = lax.broadcasted_iota(jnp.int32, (ROWS, TOK), 0)
        found = rows == ids[0:1]
        for k in range(1, TOP):
            found = found | (rows == ids[k : k + 1])
        return jnp.where(found, 1.0, 0.0).astype(BF16)

    def x_slab(j, xx):
        return ro.at[pl.ds(pl.multiple_of(j * ROWS + xx * SLAB, 16), SLAB)]

    def take_tokens(j):
        if j == 0:
            start(*z_copy(0, 1, z_fwd))
            start(*z_copy(0, 2, z_bwd))
        else:
            remote(*z_copy(j, j, z_fwd)).wait_recv()
            if j in (1, 3, 5):
                start(*z_copy(j, j + 2, z_fwd))
            elif j in (2, 4):
                start(*z_copy(j, j + 2, z_bwd))
        to = PARTNER_SLOT[j]
        start(own(j), other(to), c_send.at[to], c_recv.at[to], partner)

    def pack(j):
        remote(own(j), other(j), c_send.at[j], c_recv.at[j], partner).wait_recv()
        picker = jnp.concatenate([one_hot(row_ids(j, 0, c)), one_hot(row_ids(j, 1, 1 - c))], axis=1)
        here = pl.ds(pl.multiple_of(j * ROWS + x * SLAB, 16), SLAB)
        for at, size in chunks(width, 512):
            rows = jnp.dot(picker, tok[j, :, at : at + size], preferred_element_type=F32).astype(BF16)
            ro[here, at : at + size] = rows[0:SLAB]
            pk[j, :, at : at + size] = rows[SLAB:ROWS]
        start(pk.at[j, 0:SLAB], x_slab(j, x), x_send.at[j, 0], x_recv.at[j, 0], x_fwd)
        start(pk.at[j, SLAB : 2 * SLAB], rx.at[j], x_send.at[j, 2], x_recv.at[j, 2], x_fwd)
        start(pk.at[j, 2 * SLAB : 3 * SLAB], x_slab(j, x), x_send.at[j, 1], x_recv.at[j, 1], x_bwd)

    def x_relay(j):
        before = (x - d + 4) % 4
        remote(rx.at[j], rx.at[j], x_send.at[j, 2], x_recv.at[j, 2], x_bwd).wait_recv()
        start(rx.at[j], x_slab(j, before), x_send.at[j, 3], x_recv.at[j, 3], x_fwd)

    def y_block(i, j):
        return ry.at[i, j * ROWS : (j + 1) * ROWS]

    def send_y(j):
        for i, away in ((0, -d), (1, d), (3, 2)):
            slab = x_slab(j, (x + away + 4) % 4)
            remote(rx.at[j], slab, x_send.at[j, i], x_recv.at[j, i], x_bwd).wait_recv()
        block = ro.at[j * ROWS : (j + 1) * ROWS, 0:main]
        start(block, y_block(0, j), y_send.at[j, 0], y_recv.at[j, 0], y_fwd)
        start(block, y_block(1, j), y_send.at[j, 1], y_recv.at[j, 1], y_bwd)

    def y_relay(j):
        remote(y_block(0, j), y_block(0, j), y_send.at[j, 0], y_recv.at[j, 0], y_bwd).wait_recv()
        start(y_block(0, j), y_block(2, j), y_send.at[j, 2], y_recv.at[j, 2], y_fwd)

    def columns(at, size):
        return pl.ds(pl.multiple_of(at, 128), size)

    owners = ((y - d + 4) % 4, (y + d + 4) % 4, (y + 2) % 4)

    def compute(j):
        for i in (1, 2):
            remote(y_block(i, j), y_block(i, j), y_send.at[j, i], y_recv.at[j, i], y_bwd).wait_recv()
        if j == 0:
            for load in loads:
                load.wait()
        rows = slice(j * ROWS, (j + 1) * ROWS)

        def times(left, at, size):
            return lax.dot_general(
                left, w[:, columns(at, size)], (((1,), (1,)), ((), ())), preferred_element_type=F32
            )

        grad = times(ro[rows, 0:feats], y * feats, feats)
        for s in range(3):
            at = feats + s * EXTRA
            owner = (y + 1 + s) % 4
            grad += times(ro[rows, at : at + EXTRA], owner * feats + main, EXTRA)
        for i in range(3):
            grad += times(ry[i, rows, :], owners[i] * feats, main)

        meta = ro[rows, width - META : width].astype(F32)
        lanes = lax.broadcasted_iota(jnp.int32, (ROWS, META), 1)
        weight = (
            pltpu.roll(meta, META - 8, 1) + pltpu.roll(meta, META - 16, 1)
        ) + pltpu.roll(meta, META - 24, 1)
        chosen = (lanes < TOP) & (meta.astype(jnp.int32) == ep + 1)
        prob = jnp.sum(jnp.where(chosen, weight, 0.0), axis=1, keepdims=True)

        zz = (z + OFFSETS[j] * d + 8) % 8
        place = pl.ds(pl.multiple_of(zz * ROWS, 16), ROWS)
        gate = sg[place, :].astype(F32)
        up = su[place, :].astype(F32)
        sigmoid = jax.nn.sigmoid(gate)
        activation = gate * sigmoid
        product = activation * up
        rounded = product.astype(BF16).astype(F32)
        hs[rows, :] = (prob * product).astype(BF16)
        part = rounded * grad
        part = part[:, 0:128] + part[:, 128:256] + part[:, 256:384]
        sl_ref[pl.ds(zz, 1), :] = jnp.sum(part.T, axis=0, keepdims=True)
        scaled = prob * grad
        slope = sigmoid * (1.0 + gate * (1.0 - sigmoid))
        gg_ref[place, :] = (scaled * up * slope).astype(BF16)
        gu_ref[place, :] = (scaled * activation).astype(BF16)

    for step in range(8 + 3):
        if step < 8:
            for j in ((0,), (1, 2), (), (3, 4), (), (5, 6), (), (7,))[step]:
                take_tokens(j)
            pack(step)
        if 0 <= step - 1 < 8:
            x_relay(step - 1)
            send_y(step - 1)
        if 0 <= step - 2 < 8:
            y_relay(step - 2)
        if 0 <= step - 3 < 8:
            compute(step - 3)

    hst[...] = hs[...].T

    def weights(block, at, size):
        for piece, wide in chunks(size, 256):
            total = jnp.dot(
                hst[...], block(piece, wide), preferred_element_type=F32
            )
            gw_ref[:, columns(at + piece, wide)] = total.astype(BF16)

    weights(lambda at, size: ro[:, at : at + size], y * feats, feats)
    for s in range(3):
        owner = (y + 1 + s) % 4
        base = feats + s * EXTRA
        weights(lambda at, size: ro[:, base + at : base + at + size], owner * feats + main, EXTRA)
    for i in range(3):
        weights(lambda at, size: ry[i, :, at : at + size], owners[i] * feats, main)
    for copy in sends:
        copy.wait_send()


def slot_numbers(routes, experts):
    flat_routes = routes.reshape(-1)
    onehot = (flat_routes[:, None] == jnp.arange(experts, dtype=jnp.int32)[None, :]).astype(
        jnp.int32
    )
    earlier = jnp.cumsum(onehot, axis=0) - onehot
    return jnp.sum(earlier * onehot, axis=1).reshape(routes.shape)


def body(grad_out, routes, gates, saved_gate, saved_up, w_down):
    experts = lax.axis_size("ep")
    feats = grad_out.shape[1]
    hidden_units = saved_gate.shape[3]
    slots = experts * CAP
    width = feats + 3 * EXTRA + META
    slot_ids = slot_numbers(routes, experts)
    target = routes * CAP + slot_ids
    places = jnp.arange(slots, dtype=jnp.int32)
    matches = target[None, :, :] == places[:, None, None]

    high = lax.reduce_precision(gates, 8, 7)
    middle = lax.reduce_precision(gates - high, 8, 7)
    low = gates - high - middle
    parts = (routes.astype(F32) + 1.0, high, middle, low, slot_ids.astype(F32))
    meta = jnp.concatenate([jnp.pad(part, ((0, 0), (0, 8 - TOP))) for part in parts], axis=1)
    meta = jnp.pad(meta, ((0, 0), (0, META - 40))).astype(BF16)

    vmem = pl.BlockSpec(memory_space=pltpu.VMEM)
    hbm = pl.BlockSpec(memory_space=pl.ANY)
    dma = pltpu.SemaphoreType.DMA
    main = feats - EXTRA
    flops = 4 * slots * hidden_units * feats * NY
    grad_gate, grad_up, grad_w, slot_grad = pl.pallas_call(
        functools.partial(kernel, feats, width),
        out_shape=(
            jax.ShapeDtypeStruct((slots, hidden_units), BF16),
            jax.ShapeDtypeStruct((slots, hidden_units), BF16),
            jax.ShapeDtypeStruct((hidden_units, feats * NY), BF16),
            jax.ShapeDtypeStruct((NZ, ROWS), F32),
        ),
        in_specs=[vmem, vmem, hbm, hbm, hbm],
        out_specs=(vmem, vmem, vmem, vmem),
        scratch_shapes=[
            pltpu.VMEM((NZ, 2 * TOK, width), BF16),
            pltpu.VMEM((NZ, 3 * SLAB, width), BF16),
            pltpu.VMEM((NZ, SLAB, width), BF16),
            pltpu.VMEM((slots, width), BF16),
            pltpu.VMEM((3, slots, main), BF16),
            pltpu.VMEM((hidden_units, feats * NY), BF16),
            pltpu.VMEM((slots, hidden_units), BF16),
            pltpu.VMEM((slots, hidden_units), BF16),
            pltpu.VMEM((slots, hidden_units), BF16),
            pltpu.VMEM((hidden_units, slots), BF16),
            dma((3,)),
            dma((3,)),
            dma((3,)),
            dma((NZ,)),
            dma((NZ,)),
            dma((NZ,)),
            dma((NZ,)),
            dma((NZ, 4)),
            dma((NZ, 4)),
            dma((NZ, 3)),
            dma((NZ, 3)),
        ],
        compiler_params=pltpu.CompilerParams(
            collective_id=0, has_side_effects=True, vmem_limit_bytes=60 * 1024 * 1024
        ),
        cost_estimate=pl.CostEstimate(
            flops=flops, bytes_accessed=16 * 1024 * 1024, transcendentals=slots * hidden_units
        ),
    )(
        grad_out,
        meta,
        saved_gate.reshape(slots, hidden_units),
        saved_up.reshape(slots, hidden_units),
        w_down[0],
    )

    returned = lax.all_to_all(
        slot_grad.reshape(experts, CAP), "ep", split_axis=0, concat_axis=0, tiled=True
    )
    flat_back = returned.reshape(-1)
    picked = jnp.sum(jnp.where(matches, flat_back[:, None, None], jnp.float32(0.0)), axis=0)
    grad_gates = lax.psum(picked, "tp")
    return (
        grad_gate.reshape(saved_gate.shape),
        grad_up.reshape(saved_up.shape),
        grad_w[None],
        grad_gates,
    )


def solution(mesh):
    in_specs = (
        P("ep", "tp"),
        P("ep", None),
        P("ep", None),
        P("ep", None, None, "tp"),
        P("ep", None, None, "tp"),
        P("ep", "tp", None),
    )
    out_specs = (
        P("ep", None, None, "tp"),
        P("ep", None, None, "tp"),
        P("ep", "tp", None),
        P("ep", None),
    )
    return jax.shard_map(body, mesh=mesh, in_specs=in_specs, out_specs=out_specs, check_vma=False)
```

time: 485 us -> 214 us (0.44)
  blocking collectives: 379 us -> 7.78 us
  Pallas kernels: 0 us -> 171 us
  matrix products: 32.1 us -> 0 us
  waiting for transfers between devices: 27.7 us -> 9.24 us
  other arithmetic: 21.6 us -> 4.71 us
  between operations: 14.1 us -> 0.77 us
  local copies, waits for them, and re-layouts: 3.75 us -> 12.2 us
    all_to_all x2 -> x0, blocking collectives: 370 us -> none  [the longest x1 354 us: body(): lax.all_to_all(packed, 'ep', split_axis=0, concat_axis=0, tiled=True)]
    pallas_call x0 -> x1, Pallas kernels: none -> 171 us  [body(): pl.pallas_call(functools.partial(kernel, feats, width), out_shape=(jax.Sh...]
    dot_general x3 -> x0, matrix products: 32.1 us -> none  [the longest x1 14.9 us: body(): lax.dot_general(flat_rows, weight, (((1,), (1,)), ((), ())), preferred_el...]
    all_gather x1 -> x0, waiting for transfers between devices: 27 us -> none  [body(): gathered = lax.all_gather(grad_out, 'tp', axis=1, tiled=True)]
    convert_element_type x3 -> x0, other arithmetic: 13.8 us -> none  [the longest x1 9.12 us: body(): scaled = (flat_prob * flat_rows.astype(jnp.float32)).astype(jnp.bfloat16)]
    all_to_all x1, waiting for transfers between devices: 0.01 us -> 9.24 us  [body(): lax.all_to_all(slot_grad.reshape(experts, CAP), 'ep', split_axis=0, conca...]
    unnamed x9, local copies, waits for them, and re-layouts: 0.81 us -> 8.47 us
  transfers between devices with their start and end apart: 2 -> 1, of which waited for: 1 -> 1; matrix products, arithmetic and copies ran while one was open for 1% -> 0% of each run, Pallas kernels for 0% -> 0%
where the time goes in v1:
time: 214 us; the launch traced here: 213 us
  Pallas kernels  171 us (80%)
  local copies, waits for them, and re-layouts  12.2 us (6%)
  waiting for transfers between devices  9.24 us (4%)
  starting transfers between devices  8.04 us (4%)
  blocking collectives  7.78 us (4%)
  other arithmetic  4.71 us (2%)
    pallas_call x1, Pallas kernels, body(): pl.pallas_call(functools.partial(kernel, feats, width), out_shape=(jax.Sh...  171 us
    all_to_all x1, waiting for transfers between devices, body(): lax.all_to_all(slot_grad.reshape(experts, CAP), 'ep', split_axis=0, conca...  9.24 us
    unnamed x9, local copies, waits for them, and re-layouts  8.47 us
    all_to_all x1, starting transfers between devices, body(): lax.all_to_all(slot_grad.reshape(experts, CAP), 'ep', split_axis=0, conca...  8.04 us
    psum x1, blocking collectives, body(): grad_gates = lax.psum(picked, 'tp')  7.78 us
  transfers between devices with their start and end apart: 1, of which 1 were waited for; matrix products, arithmetic and copies ran while one was open for 0% of the time, Pallas kernels for 0%

profile of v1, /device:TPU:1, one launch (start us, length us, event | category | flops | bytes accessed | tf_op | source)
XLA Modules:
  0.0 213.3 jit_solution(10391526913236719641)
XLA Ops:
  0.6 0.7 add_convert_fusion
  1.3 0.8 copy.48
  2.1 0.1 eq.42
  2.3 0.1 eq.38
  2.4 0.7 reduce_precision.6
  3.1 0.8 copy.46
  3.9 0.1 copy.44
  4.0 0.1 copy.45
  4.2 1.8 reduce-window.6
  6.1 0.3 slice_reduce_fusion
  6.4 0.1 fusion.2
  6.5 0.1 reshape.48
  6.7 0.1 concatenate.4
  6.8 0.6 pad.31.meta_ref
  7.4 0.0 copy-start.1
  7.4 170.6 %shard_map.93 = (bf16[1536,384]{1,0:T(8,128)(2,1)}, bf16[1536,384]{1,0:T(8,128)(2,1)}, bf16[384,5120]{1,0:T(8,128)(2,1)}, f32[8,192]{1,0:T(8,128)}) custom-call(bf16[128,1280]{1,0:T(8,128)(2,1)} %tok_ref.1, bf16[128,128]{1,0:T(8,128)(2,1)} %pad.31.meta_ref, bf16[1536,384]{1,0:T(8,128)(2,1)} %bitcast.32, bf16[1536,384]{1,0:T(8,128)(2,1)} %bitcast.33, ...), custom_call_target="tpu_custom_call" | custom-call | flops 12079595520 | bytes 16777216 | tf_op jit(solution)/shard_map/pallas_call | solution.py:311
  178.0 1.4 all_to_all.6
  179.4 8.0 %all-to-all-start = ((f32[64,1,24]{2,1,0:T(1,128)}), f32[64,1,24]{2,1,0:T(1,128)S(1)}, u32[]{:S(2)}, u32[]{:S(2)}) async-start(f32[64,1,24]{2,1,0:T(1,128)} %bitcast.7), calls=%async_computation | async-start | bytes 65536 | tf_op jit(solution)/shard_map/all_to_all | solution.py:358
  187.4 0.1 copy.51
  187.5 0.0 copy-done.1
  187.5 9.2 %all-to-all-done = f32[64,1,24]{2,1,0:T(1,128)S(1)} async-done(((f32[64,1,24]{2,1,0:T(1,128)}), f32[64,1,24]{2,1,0:T(1,128)S(1)}, u32[]{:S(2)}, u32[]{:S(2)}) %all-to-all-start) | async-done | bytes 6176 | tf_op jit(solution)/shard_map/all_to_all | solution.py:358
  196.7 0.5 broadcast.35
  197.2 0.7 reduce.5
  198.0 0.1 broadcast_in_dim.21
  198.1 0.6 select_reduce_fusion
  198.7 7.8 %psum.7 = f32[128,6]{0,1:T(8,128)} all-reduce(f32[128,6]{0,1:T(8,128)S(1)} %select_reduce_fusion), channel_id=1, replica_groups=mesh['tp'=4,'ep'=64] {'tp'}, use_global_device_ids=true, to_apply=%region_4.5 | all-reduce | flops 768 | bytes 6144 | tf_op jit(solution)/shard_map/psum | solution.py:363
  206.4 0.0 copy-start
  206.4 2.6 %copy.58 = bf16[1,64,24,384]{3,2,1,0:T(8,128)(2,1)} copy(bf16[1,64,24,384]{3,2,1,0:T(8,128)(2,1)} %bitcast.29) | data formatting | bytes 2359296
  209.0 2.4 %copy.59 = bf16[1,64,24,384]{3,2,1,0:T(8,128)(2,1)} copy(bf16[1,64,24,384]{3,2,1,0:T(8,128)(2,1)} %bitcast.28) | data formatting | bytes 2359296
  211.4 0.0 copy-done
  211.4 1.9 copy.60
  (10 shorter events, 0.1 us)
Async XLA Ops:
  7.4 180.1 %copy-start.1 = (s32[128,6]{0,1:T(8,128)S(1)}, s32[128,6]{0,1:T(8,128)}, u32[]{:S(2)}) copy-start(s32[128,6]{0,1:T(8,128)} %param.7) | copy-start | bytes 9220
  179.4 17.3 %all-to-all-start = ((f32[64,1,24]{2,1,0:T(1,128)}), f32[64,1,24]{2,1,0:T(1,128)S(1)}, u32[]{:S(2)}, u32[]{:S(2)}) async-start(f32[64,1,24]{2,1,0:T(1,128)} %bitcast.7), calls=%async_computation | async-start | bytes 65536 | tf_op jit(solution)/shard_map/all_to_all | solution.py:358
  206.4 5.0 %copy-start = (bf16[384,5120]{1,0:T(8,128)(2,1)S(1)}, bf16[384,5120]{1,0:T(8,128)(2,1)}, u32[]{:S(2)}) copy-start(bf16[384,5120]{1,0:T(8,128)(2,1)} %get-tuple-element.10) | copy-start | bytes 11796484

commit v2 on v1

--- a/solution.py
+++ b/solution.py
@@ -9,13 +9,18 @@
 
 NZ, NX, NY = 8, 4, 4
 CAP = 24
+EXPERTS = 64
 TOK = 128
 TOP = 6
-EXTRA = 256
+EXTRA = 384
 META = 128
 SLAB = 2 * CAP
 ROWS = NX * SLAB
 PARTNER_SLOT = (0, 2, 1, 4, 3, 6, 5, 7)
+ORDER = (
+    "T0 P0 Y0 T1 T2 P1 P2 Y1 R0 T3 T4 P3 Y2 R1 C0 P4 Y3 R2 C1 T5 T6 P5 Y4 R3 C2 "
+    "P6 Y5 R4 C3 T7 P7 Y6 R5 C4 Y7 R6 C5 R7 C6 C7"
+)
 OFFSETS = (0, -1, 1, -2, 2, -3, 3, -4)
 F32 = jnp.float32
 BF16 = jnp.bfloat16
@@ -30,17 +35,17 @@
     feats,
     width,
     tok_ref,
-    meta_ref,
+    routes_ref,
+    gates_ref,
     gate_hbm,
     up_hbm,
     w_hbm,
     gg_ref,
     gu_ref,
     gw_ref,
-    sl_ref,
+    back_ref,
     tok,
     pk,
-    rx,
     ro,
     ry,
     w,
@@ -48,6 +53,12 @@
     su,
     hs,
     hst,
+    table,
+    sl,
+    sums,
+    theirs,
+    zs,
+    zr,
     in_sem,
     e_send,
     e_recv,
@@ -59,6 +70,10 @@
     x_recv,
     y_send,
     y_recv,
+    s_send,
+    s_recv,
+    b_send,
+    b_recv,
 ):
     y = lax.axis_index("tp")
     ep = lax.axis_index("ep")
@@ -73,11 +88,14 @@
 
     z_fwd, z_bwd = ep_at((z + d + 8) % 8, x, c), ep_at((z - d + 8) % 8, x, c)
     x_fwd, x_bwd = ep_at(z, (x + d + 4) % 4, c), ep_at(z, (x - d + 4) % 4, c)
+    x_far = ep_at(z, (x + 2) % 4, c)
+    y_far = {"tp": (y + 2) % 4}
     y_fwd, y_bwd = {"tp": (y + d + 4) % 4}, {"tp": (y - d + 4) % 4}
     partner = ep_at(z, x, 1 - c)
 
     barrier = pltpu.get_barrier_semaphore()
-    for peer in (z_fwd, z_bwd, x_fwd, x_bwd, y_fwd, y_bwd, partner):
+    z_far = [ep_at((z + o) % 8, x, c) for o in range(2, 7)]
+    for peer in [z_fwd, z_bwd, x_fwd, x_far, x_bwd, y_fwd, y_far, y_bwd, partner] + z_far:
         pl.semaphore_signal(barrier, inc=1, device_id=peer, device_id_type=MESH)
 
     loads = [
@@ -88,8 +106,33 @@
     for load in loads:
         load.start()
     tok[0, 0:TOK, 0:feats] = tok_ref[...]
-    tok[0, 0:TOK, width - META : width] = meta_ref[...]
-    pl.semaphore_wait(barrier, 7)
+    table[...] = jnp.zeros((META, TOK), F32)
+    table[0:TOP] = routes_ref[...].astype(F32) + 1.0
+    gates = gates_ref[...]
+    high = gates.astype(BF16).astype(F32)
+    middle = (gates - high).astype(BF16).astype(F32)
+    table[8 : 8 + TOP] = high
+    table[16 : 16 + TOP] = middle
+    table[24 : 24 + TOP] = (gates - high) - middle
+    named = table[0:8].astype(jnp.int32)
+    numbers = lax.broadcasted_iota(jnp.int32, (EXPERTS, TOK), 0) + 1
+    chosen_by = [numbers == named[k : k + 1] for k in range(TOP)]
+    used = jnp.where(chosen_by[0], 1.0, 0.0)
+    for k in range(1, TOP):
+        used += jnp.where(chosen_by[k], 1.0, 0.0)
+    order = lax.broadcasted_iota(jnp.int32, (TOK, TOK), 0) < lax.broadcasted_iota(
+        jnp.int32, (TOK, TOK), 1
+    )
+    earlier = jnp.dot(
+        used.astype(BF16), jnp.where(order, 1.0, 0.0).astype(BF16), preferred_element_type=F32
+    )
+    for k in range(TOP):
+        table[32 + k : 33 + k] = jnp.sum(
+            jnp.where(chosen_by[k], earlier, 0.0), axis=0, keepdims=True
+        )
+    tok[0, 0:TOK, width - META : width] = table[...].T.astype(BF16)
+    sl[...] = jnp.zeros(sl.shape, F32)
+    pl.semaphore_wait(barrier, 14)
 
     sends = []
 
@@ -168,22 +211,17 @@
             rows = jnp.dot(picker, tok[j, :, at : at + size], preferred_element_type=F32).astype(BF16)
             ro[here, at : at + size] = rows[0:SLAB]
             pk[j, :, at : at + size] = rows[SLAB:ROWS]
-        start(pk.at[j, 0:SLAB], x_slab(j, x), x_send.at[j, 0], x_recv.at[j, 0], x_fwd)
-        start(pk.at[j, SLAB : 2 * SLAB], rx.at[j], x_send.at[j, 2], x_recv.at[j, 2], x_fwd)
-        start(pk.at[j, 2 * SLAB : 3 * SLAB], x_slab(j, x), x_send.at[j, 1], x_recv.at[j, 1], x_bwd)
-
-    def x_relay(j):
-        before = (x - d + 4) % 4
-        remote(rx.at[j], rx.at[j], x_send.at[j, 2], x_recv.at[j, 2], x_bwd).wait_recv()
-        start(rx.at[j], x_slab(j, before), x_send.at[j, 3], x_recv.at[j, 3], x_fwd)
+        for i, peer in enumerate((x_fwd, x_far, x_bwd)):
+            slab = pk.at[j, i * SLAB : (i + 1) * SLAB]
+            start(slab, x_slab(j, x), x_send.at[j, i], x_recv.at[j, i], peer)
 
     def y_block(i, j):
         return ry.at[i, j * ROWS : (j + 1) * ROWS]
 
     def send_y(j):
-        for i, away in ((0, -d), (1, d), (3, 2)):
+        for i, away in enumerate((-d, 2, d)):
             slab = x_slab(j, (x + away + 4) % 4)
-            remote(rx.at[j], slab, x_send.at[j, i], x_recv.at[j, i], x_bwd).wait_recv()
+            remote(slab, slab, x_send.at[j, i], x_recv.at[j, i], x_bwd).wait_recv()
         block = ro.at[j * ROWS : (j + 1) * ROWS, 0:main]
         start(block, y_block(0, j), y_send.at[j, 0], y_recv.at[j, 0], y_fwd)
         start(block, y_block(1, j), y_send.at[j, 1], y_recv.at[j, 1], y_bwd)
@@ -237,52 +275,90 @@
         hs[rows, :] = (prob * product).astype(BF16)
         part = rounded * grad
         part = part[:, 0:128] + part[:, 128:256] + part[:, 256:384]
-        sl_ref[pl.ds(zz, 1), :] = jnp.sum(part.T, axis=0, keepdims=True)
+        sl[y, pl.ds(zz, 1), 0:ROWS] = jnp.sum(part.T, axis=0, keepdims=True)
         scaled = prob * grad
         slope = sigmoid * (1.0 + gate * (1.0 - sigmoid))
         gg_ref[place, :] = (scaled * up * slope).astype(BF16)
         gu_ref[place, :] = (scaled * activation).astype(BF16)
 
-    for step in range(8 + 3):
-        if step < 8:
-            for j in ((0,), (1, 2), (), (3, 4), (), (5, 6), (), (7,))[step]:
-                take_tokens(j)
-            pack(step)
-        if 0 <= step - 1 < 8:
-            x_relay(step - 1)
-            send_y(step - 1)
-        if 0 <= step - 2 < 8:
-            y_relay(step - 2)
-        if 0 <= step - 3 < 8:
-            compute(step - 3)
+    stage = {"T": take_tokens, "P": pack, "Y": send_y, "R": y_relay, "C": compute}
+    for name in ORDER.split():
+        stage[name[0]](int(name[1]))
+
+    def wait(ref, sem):
+        remote(ref, ref, s_send.at[0], sem, y_bwd).wait_recv()
+
+    for i, peer in enumerate((y_fwd, y_far, y_bwd)):
+        start(sl.at[y], sl.at[y], s_send.at[i], s_recv.at[i], peer)
 
     hst[...] = hs[...].T
 
     def weights(block, at, size):
         for piece, wide in chunks(size, 256):
-            total = jnp.dot(
-                hst[...], block(piece, wide), preferred_element_type=F32
-            )
+            total = jnp.dot(hst[...], block(piece, wide), preferred_element_type=F32)
             gw_ref[:, columns(at + piece, wide)] = total.astype(BF16)
 
     weights(lambda at, size: ro[:, at : at + size], y * feats, feats)
+
+    for i, away in enumerate((-d, 2, d)):
+        wait(sl.at[(y + away + 4) % 4], s_recv.at[i])
+    sums[x] = ((sl[0] + sl[1]) + sl[2]) + sl[3]
+    for i, peer in enumerate((x_fwd, x_far, x_bwd)):
+        start(sums.at[x], sums.at[x], s_send.at[3 + i], s_recv.at[3 + i], peer)
+
     for s in range(3):
         owner = (y + 1 + s) % 4
         base = feats + s * EXTRA
         weights(lambda at, size: ro[:, base + at : base + at + size], owner * feats + main, EXTRA)
-    for i in range(3):
+
+    for i, away in enumerate((-d, 2, d)):
+        wait(sums.at[(x + away + 4) % 4], s_recv.at[3 + i])
+    start(sums, theirs, s_send.at[6], s_recv.at[6], partner)
+
+    weights(lambda at, size: ry[0, :, at : at + size], owners[0] * feats, main)
+
+    wait(theirs, s_recv.at[6])
+    shift = (256 - (x * SLAB + c * CAP)) % 256
+    for i in range(NX):
+        for core in range(2):
+            block = jnp.where(c == core, sums[i], theirs[i])
+            zs[:, 2 * i + core, :] = pltpu.roll(block, shift, 1)[:, 0:128]
+    for o in range(1, NZ):
+        start(
+            zs.at[(z + o) % 8],
+            zr.at[z],
+            b_send.at[o],
+            b_recv.at[o],
+            ep_at((z + o) % 8, x, c),
+        )
+    zr[z] = zs[z]
+
+    for i in range(1, 3):
         weights(lambda at, size: ry[i, :, at : at + size], owners[i] * feats, main)
+
+    for o in range(1, NZ):
+        wait(zr.at[(z - o + 8) % 8], b_recv.at[o])
+    back = zr[...].reshape(EXPERTS, 128)
+    high = back.astype(BF16)
+    rest = back - high.astype(F32)
+    middle = rest.astype(BF16)
+    low = (rest - middle.astype(F32)).astype(BF16)
+    numbers = lax.broadcasted_iota(jnp.int32, (EXPERTS, TOK), 0) + 1
+    slots = lax.broadcasted_iota(jnp.int32, (128, TOK), 0)
+    named = table[0:8].astype(jnp.int32)
+    wanted = table[32:40].astype(jnp.int32)
+    for k in range(TOP):
+        picker = jnp.where(numbers == named[k : k + 1], 1.0, 0.0).astype(BF16)
+        total = jnp.zeros((128, TOK), F32)
+        for part in (high, middle, low):
+            total += lax.dot_general(
+                part, picker, (((0,), (0,)), ((), ())), preferred_element_type=F32
+            )
+        back_ref[k : k + 1, :] = jnp.sum(
+            jnp.where(slots == wanted[k : k + 1], total, 0.0), axis=0, keepdims=True
+        )
     for copy in sends:
         copy.wait_send()
-
-
-def slot_numbers(routes, experts):
-    flat_routes = routes.reshape(-1)
-    onehot = (flat_routes[:, None] == jnp.arange(experts, dtype=jnp.int32)[None, :]).astype(
-        jnp.int32
-    )
-    earlier = jnp.cumsum(onehot, axis=0) - onehot
-    return jnp.sum(earlier * onehot, axis=1).reshape(routes.shape)
 
 
 def body(grad_out, routes, gates, saved_gate, saved_up, w_down):
@@ -291,37 +367,25 @@
     hidden_units = saved_gate.shape[3]
     slots = experts * CAP
     width = feats + 3 * EXTRA + META
-    slot_ids = slot_numbers(routes, experts)
-    target = routes * CAP + slot_ids
-    places = jnp.arange(slots, dtype=jnp.int32)
-    matches = target[None, :, :] == places[:, None, None]
-
-    high = lax.reduce_precision(gates, 8, 7)
-    middle = lax.reduce_precision(gates - high, 8, 7)
-    low = gates - high - middle
-    parts = (routes.astype(F32) + 1.0, high, middle, low, slot_ids.astype(F32))
-    meta = jnp.concatenate([jnp.pad(part, ((0, 0), (0, 8 - TOP))) for part in parts], axis=1)
-    meta = jnp.pad(meta, ((0, 0), (0, META - 40))).astype(BF16)
 
     vmem = pl.BlockSpec(memory_space=pltpu.VMEM)
     hbm = pl.BlockSpec(memory_space=pl.ANY)
     dma = pltpu.SemaphoreType.DMA
     main = feats - EXTRA
     flops = 4 * slots * hidden_units * feats * NY
-    grad_gate, grad_up, grad_w, slot_grad = pl.pallas_call(
+    grad_gate, grad_up, grad_w, back = pl.pallas_call(
         functools.partial(kernel, feats, width),
         out_shape=(
             jax.ShapeDtypeStruct((slots, hidden_units), BF16),
             jax.ShapeDtypeStruct((slots, hidden_units), BF16),
             jax.ShapeDtypeStruct((hidden_units, feats * NY), BF16),
-            jax.ShapeDtypeStruct((NZ, ROWS), F32),
+            jax.ShapeDtypeStruct((TOP, TOK), F32),
         ),
-        in_specs=[vmem, vmem, hbm, hbm, hbm],
+        in_specs=[vmem, vmem, vmem, hbm, hbm, hbm],
         out_specs=(vmem, vmem, vmem, vmem),
         scratch_shapes=[
             pltpu.VMEM((NZ, 2 * TOK, width), BF16),
             pltpu.VMEM((NZ, 3 * SLAB, width), BF16),
-            pltpu.VMEM((NZ, SLAB, width), BF16),
             pltpu.VMEM((slots, width), BF16),
             pltpu.VMEM((3, slots, main), BF16),
             pltpu.VMEM((hidden_units, feats * NY), BF16),
@@ -329,6 +393,12 @@
             pltpu.VMEM((slots, hidden_units), BF16),
             pltpu.VMEM((slots, hidden_units), BF16),
             pltpu.VMEM((hidden_units, slots), BF16),
+            pltpu.VMEM((META, TOK), F32),
+            pltpu.VMEM((NY, NZ, 256), F32),
+            pltpu.VMEM((NX, NZ, 256), F32),
+            pltpu.VMEM((NX, NZ, 256), F32),
+            pltpu.VMEM((NZ, 8, 128), F32),
+            pltpu.VMEM((NZ, 8, 128), F32),
             dma((3,)),
             dma((3,)),
             dma((3,)),
@@ -336,10 +406,14 @@
             dma((NZ,)),
             dma((NZ,)),
             dma((NZ,)),
-            dma((NZ, 4)),
-            dma((NZ, 4)),
             dma((NZ, 3)),
             dma((NZ, 3)),
+            dma((NZ, 3)),
+            dma((NZ, 3)),
+            dma((7,)),
+            dma((7,)),
+            dma((NZ,)),
+            dma((NZ,)),
         ],
         compiler_params=pltpu.CompilerParams(
             collective_id=0, has_side_effects=True, vmem_limit_bytes=60 * 1024 * 1024
@@ -349,23 +423,18 @@
         ),
     )(
         grad_out,
-        meta,
+        routes.T,
+        gates.T,
         saved_gate.reshape(slots, hidden_units),
         saved_up.reshape(slots, hidden_units),
         w_down[0],
     )
 
-    returned = lax.all_to_all(
-        slot_grad.reshape(experts, CAP), "ep", split_axis=0, concat_axis=0, tiled=True
-    )
-    flat_back = returned.reshape(-1)
-    picked = jnp.sum(jnp.where(matches, flat_back[:, None, None], jnp.float32(0.0)), axis=0)
-    grad_gates = lax.psum(picked, "tp")
     return (
         grad_gate.reshape(saved_gate.shape),
         grad_up.reshape(saved_up.shape),
         grad_w[None],
-        grad_gates,
+        back.T,
     )
 
 

time: 214 us -> 160 us (0.75)
  Pallas kernels: 171 us -> 151 us
  waiting for transfers between devices: 9.24 us -> 0 us
  starting transfers between devices: 8.04 us -> 0 us
  blocking collectives: 7.78 us -> 0 us
  local copies, waits for them, and re-layouts: 12.2 us -> 7.48 us
  other arithmetic: 4.71 us -> 0 us
    pallas_call x1, Pallas kernels: 171 us -> 151 us  [body(): pl.pallas_call(functools.partial(kernel, feats, width), out_shape=(jax.Sh...]
    all_to_all x1 -> x0, waiting for transfers between devices: 9.24 us -> none  [body(): lax.all_to_all(slot_grad.reshape(experts, CAP), 'ep', split_axis=0, conca...]
    all_to_all x1 -> x0, starting transfers between devices: 8.04 us -> none  [body(): lax.all_to_all(slot_grad.reshape(experts, CAP), 'ep', split_axis=0, conca...]
    psum x1 -> x0, blocking collectives: 7.78 us -> none  [body(): grad_gates = lax.psum(picked, 'tp')]
    another operation x5 -> x0, other arithmetic: 2.54 us -> none
    unnamed x9 -> x8, local copies, waits for them, and re-layouts: 8.47 us -> 7.48 us
  transfers between devices with their start and end apart: 1 -> 0, of which waited for: 1 -> 0; matrix products, arithmetic and copies ran while one was open for 0% -> 0% of each run, Pallas kernels for 0% -> 0%
where the time goes in v2:
time: 160 us; the launch traced here: 159 us
  Pallas kernels  151 us (94%)
  local copies, waits for them, and re-layouts  7.48 us (5%)
    pallas_call x1, Pallas kernels, body(): pl.pallas_call(functools.partial(kernel, feats, width), out_shape=(jax.Sh...  151 us
    unnamed x8, local copies, waits for them, and re-layouts  7.48 us

profile of v2, /device:TPU:1, one launch (start us, length us, event | category | flops | bytes accessed | tf_op | source)
XLA Modules:
  0.0 159.4 jit_solution(10919052591884591021)
XLA Ops:
  0.6 151.3 %shard_map.93 = (bf16[1536,384]{1,0:T(8,128)(2,1)}, bf16[1536,384]{1,0:T(8,128)(2,1)}, bf16[384,5120]{1,0:T(8,128)(2,1)}, f32[6,128]{1,0:T(8,128)}) custom-call(bf16[128,1280]{1,0:T(8,128)(2,1)} %tok_ref.1, s32[6,128]{1,0:T(8,128)} %bitcast.16, f32[6,128]{1,0:T(8,128)} %bitcast.17, bf16[1536,384]{1,0:T(8,128)(2,1)} %bitcast.14, bf16[1536,384]{1,0:T(8,128)(2,1)} %bitcast.15, ...), custom_call_target="tpu_custom_call" | custom-call | flops 12079595520 | bytes 16777216 | tf_op jit(solution)/shard_map/pallas_call | solution.py:376
  152.0 0.0 copy-start
  152.0 2.6 %copy.14 = bf16[1,64,24,384]{3,2,1,0:T(8,128)(2,1)} copy(bf16[1,64,24,384]{3,2,1,0:T(8,128)(2,1)} %bitcast.11) | data formatting | bytes 2359296
  154.5 2.4 %copy.15 = bf16[1,64,24,384]{3,2,1,0:T(8,128)(2,1)} copy(bf16[1,64,24,384]{3,2,1,0:T(8,128)(2,1)} %bitcast.10) | data formatting | bytes 2359296
  156.9 0.0 copy-done
  156.9 0.0 copy-start.1
  156.9 1.9 %copy.16 = bf16[1,384,5120]{2,1,0:T(8,128)(2,1)} copy(bf16[1,384,5120]{2,1,0:T(8,128)(2,1)S(1)} %bitcast.9) | data formatting | bytes 7864320
  158.8 0.0 copy-done.1
  158.8 0.6 copy.17
Async XLA Ops:
  152.0 5.0 %copy-start = (bf16[384,5120]{1,0:T(8,128)(2,1)S(1)}, bf16[384,5120]{1,0:T(8,128)(2,1)}, u32[]{:S(2)}) copy-start(bf16[384,5120]{1,0:T(8,128)(2,1)} %get-tuple-element.10) | copy-start | bytes 11796484
  156.9 1.9 %copy-start.1 = (f32[6,128]{1,0:T(8,128)S(1)}, f32[6,128]{1,0:T(8,128)}, u32[]{:S(2)}) copy-start(f32[6,128]{1,0:T(8,128)} %get-tuple-element.11) | copy-start | bytes 9220

commit v3 on v2

--- a/solution.py
+++ b/solution.py
@@ -15,10 +15,11 @@
 EXTRA = 384
 META = 128
 SLAB = 2 * CAP
+PARTS = 4
 ROWS = NX * SLAB
 PARTNER_SLOT = (0, 2, 1, 4, 3, 6, 5, 7)
 ORDER = (
-    "T0 P0 Y0 T1 T2 P1 P2 Y1 R0 T3 T4 P3 Y2 R1 C0 P4 Y3 R2 C1 T5 T6 P5 Y4 R3 C2 "
+    "P0 Y0 T1 T2 P1 P2 Y1 R0 T3 T4 P3 Y2 R1 C0 P4 Y3 R2 C1 T5 T6 P5 Y4 R3 C2 "
     "P6 Y5 R4 C3 T7 P7 Y6 R5 C4 Y7 R6 C5 R7 C6 C7"
 )
 OFFSETS = (0, -1, 1, -2, 2, -3, 3, -4)
@@ -40,9 +41,9 @@
     gate_hbm,
     up_hbm,
     w_hbm,
-    gg_ref,
-    gu_ref,
-    gw_ref,
+    gg_hbm,
+    gu_hbm,
+    gw_hbm,
     back_ref,
     tok,
     pk,
@@ -53,6 +54,9 @@
     su,
     hs,
     hst,
+    gg,
+    gu,
+    gw,
     table,
     sl,
     sums,
@@ -60,6 +64,8 @@
     zs,
     zr,
     in_sem,
+    o_sem,
+    w_sem,
     e_send,
     e_recv,
     z_send,
@@ -82,6 +88,7 @@
     c = ep % 2
     d = 1 - 2 * c
     main = feats - EXTRA
+    extras = feats + META
 
     def ep_at(zz, xx, cc):
         return {"ep": zz * 8 + xx * 2 + cc}
@@ -130,7 +137,7 @@
         table[32 + k : 33 + k] = jnp.sum(
             jnp.where(chosen_by[k], earlier, 0.0), axis=0, keepdims=True
         )
-    tok[0, 0:TOK, width - META : width] = table[...].T.astype(BF16)
+    tok[0, 0:TOK, feats : feats + META] = table[...].T.astype(BF16)
     sl[...] = jnp.zeros(sl.shape, F32)
     pl.semaphore_wait(barrier, 14)
 
@@ -152,16 +159,15 @@
         sends.append(copy)
 
     def extra_at(slot):
-        return tok.at[0, 0:TOK, pl.ds(pl.multiple_of(feats + slot * EXTRA, 128), EXTRA)]
-
-    from_bwd, from_fwd = (3 - d) % 4, (3 + d) % 4
+        return tok.at[0, 0:TOK, pl.ds(pl.multiple_of(extras + slot * EXTRA, 128), EXTRA)]
+
+    here = tok.at[0, 0:TOK, 0:extras]
+    for j, peer in ((1, z_fwd), (2, z_bwd)):
+        start(here, tok.at[j, 0:TOK, 0:extras], z_send.at[j], z_recv.at[j], peer)
     mine = tok_ref.at[:, main:feats]
-    start(mine, extra_at(from_bwd), e_send.at[0], e_recv.at[0], y_fwd)
-    start(mine, extra_at(from_fwd), e_send.at[1], e_recv.at[1], y_bwd)
-    remote(mine, extra_at(from_bwd), e_send.at[0], e_recv.at[0], y_bwd).wait_recv()
-    start(extra_at(from_bwd), extra_at(1), e_send.at[2], e_recv.at[2], y_fwd)
-    remote(mine, extra_at(from_fwd), e_send.at[1], e_recv.at[1], y_fwd).wait_recv()
-    remote(mine, extra_at(1), e_send.at[2], e_recv.at[2], y_bwd).wait_recv()
+    slots = ((3 - d) % 4, 1, (3 + d) % 4)
+    for i, peer in enumerate((y_fwd, y_far, y_bwd)):
+        start(mine, extra_at(slots[i]), e_send.at[i], e_recv.at[i], peer)
 
     def own(j):
         return tok.at[j, 0:TOK]
@@ -173,7 +179,7 @@
         return (own(src), own(dst), z_send.at[dst], z_recv.at[dst], peer)
 
     def row_ids(j, half, core):
-        table = tok[j, half * TOK : (half + 1) * TOK, width - META : width].astype(F32).T
+        table = tok[j, half * TOK : (half + 1) * TOK, feats : feats + META].astype(F32).T
         expert = table[0:8].astype(jnp.int32) - 1
         slot = table[32:40].astype(jnp.int32)
         hit = (lax.shift_right_arithmetic(expert, 3) == z) & ((expert & 1) == c)
@@ -190,38 +196,69 @@
     def x_slab(j, xx):
         return ro.at[pl.ds(pl.multiple_of(j * ROWS + xx * SLAB, 16), SLAB)]
 
+    def exchange(part, sem):
+        return (
+            tok.at[0, 0:TOK, part],
+            tok.at[0, TOK : 2 * TOK, part],
+            c_send.at[sem],
+            c_recv.at[sem],
+            partner,
+        )
+
     def take_tokens(j):
-        if j == 0:
-            start(*z_copy(0, 1, z_fwd))
-            start(*z_copy(0, 2, z_bwd))
+        if j in (1, 2):
+            for part, sem in ((slice(0, extras), z_recv.at[j]), (slice(extras, width), e_recv.at[2 + j])):
+                ref = tok.at[j, 0:TOK, part]
+                remote(ref, ref, z_send.at[j], sem, z_fwd).wait_recv()
         else:
             remote(*z_copy(j, j, z_fwd)).wait_recv()
-            if j in (1, 3, 5):
-                start(*z_copy(j, j + 2, z_fwd))
-            elif j in (2, 4):
-                start(*z_copy(j, j + 2, z_bwd))
+        if j in (1, 3, 5):
+            start(*z_copy(j, j + 2, z_fwd))
+        elif j in (2, 4):
+            start(*z_copy(j, j + 2, z_bwd))
         to = PARTNER_SLOT[j]
         start(own(j), other(to), c_send.at[to], c_recv.at[to], partner)
 
+    pieces = (slice(0, main), slice(main, width))
+
     def pack(j):
-        remote(own(j), other(j), c_send.at[j], c_recv.at[j], partner).wait_recv()
+        if j > 0:
+            remote(own(j), other(j), c_send.at[j], c_recv.at[j], partner).wait_recv()
+        else:
+            start(*exchange(slice(0, extras), 0))
+            remote(*exchange(slice(0, extras), 0)).wait_recv()
         picker = jnp.concatenate([one_hot(row_ids(j, 0, c)), one_hot(row_ids(j, 1, 1 - c))], axis=1)
         here = pl.ds(pl.multiple_of(j * ROWS + x * SLAB, 16), SLAB)
-        for at, size in chunks(width, 512):
-            rows = jnp.dot(picker, tok[j, :, at : at + size], preferred_element_type=F32).astype(BF16)
-            ro[here, at : at + size] = rows[0:SLAB]
-            pk[j, :, at : at + size] = rows[SLAB:ROWS]
-        for i, peer in enumerate((x_fwd, x_far, x_bwd)):
-            slab = pk.at[j, i * SLAB : (i + 1) * SLAB]
-            start(slab, x_slab(j, x), x_send.at[j, i], x_recv.at[j, i], peer)
+        for p, piece in enumerate(pieces):
+            if j == 0 and p == 1:
+                for i in range(3):
+                    remote(mine, extra_at(slots[i]), e_send.at[i], e_recv.at[i], y_bwd).wait_recv()
+                gathered = tok.at[0, 0:TOK, extras:width]
+                for k, peer in ((1, z_fwd), (2, z_bwd)):
+                    part = tok.at[k, 0:TOK, extras:width]
+                    start(gathered, part, e_send.at[2 + k], e_recv.at[2 + k], peer)
+                start(*exchange(slice(extras, width), NZ))
+                remote(*exchange(slice(extras, width), NZ)).wait_recv()
+            for at, size in chunks(piece.stop - piece.start, 512):
+                columns = slice(piece.start + at, piece.start + at + size)
+                rows = jnp.dot(picker, tok[j, :, columns], preferred_element_type=F32).astype(BF16)
+                ro[here, columns] = rows[0:SLAB]
+                pk[j, :, columns] = rows[SLAB:ROWS]
+            for i, peer in enumerate((x_fwd, x_far, x_bwd)):
+                slab = pk.at[j, i * SLAB : (i + 1) * SLAB, piece]
+                sem = 3 * p + i
+                start(slab, x_slab(j, x).at[:, piece], x_send.at[j, sem], x_recv.at[j, sem], peer)
+
+    def wait_x(j, p):
+        for i, away in enumerate((-d, 2, d)):
+            slab = x_slab(j, (x + away + 4) % 4).at[:, pieces[p]]
+            remote(slab, slab, x_send.at[j, i], x_recv.at[j, 3 * p + i], x_bwd).wait_recv()
 
     def y_block(i, j):
         return ry.at[i, j * ROWS : (j + 1) * ROWS]
 
     def send_y(j):
-        for i, away in enumerate((-d, 2, d)):
-            slab = x_slab(j, (x + away + 4) % 4)
-            remote(slab, slab, x_send.at[j, i], x_recv.at[j, i], x_bwd).wait_recv()
+        wait_x(j, 0)
         block = ro.at[j * ROWS : (j + 1) * ROWS, 0:main]
         start(block, y_block(0, j), y_send.at[j, 0], y_recv.at[j, 0], y_fwd)
         start(block, y_block(1, j), y_send.at[j, 1], y_recv.at[j, 1], y_bwd)
@@ -230,17 +267,23 @@
         remote(y_block(0, j), y_block(0, j), y_send.at[j, 0], y_recv.at[j, 0], y_bwd).wait_recv()
         start(y_block(0, j), y_block(2, j), y_send.at[j, 2], y_recv.at[j, 2], y_fwd)
 
+    stores = []
+
+    def store(src, dst, sem):
+        copy = pltpu.make_async_copy(src, dst, sem)
+        copy.start()
+        stores.append(copy)
+
     def columns(at, size):
         return pl.ds(pl.multiple_of(at, 128), size)
 
     owners = ((y - d + 4) % 4, (y + d + 4) % 4, (y + 2) % 4)
 
     def compute(j):
-        for i in (1, 2):
-            remote(y_block(i, j), y_block(i, j), y_send.at[j, i], y_recv.at[j, i], y_bwd).wait_recv()
         if j == 0:
             for load in loads:
                 load.wait()
+        wait_x(j, 1)
         rows = slice(j * ROWS, (j + 1) * ROWS)
 
         def times(left, at, size):
@@ -250,13 +293,16 @@
 
         grad = times(ro[rows, 0:feats], y * feats, feats)
         for s in range(3):
-            at = feats + s * EXTRA
+            at = extras + s * EXTRA
             owner = (y + 1 + s) % 4
             grad += times(ro[rows, at : at + EXTRA], owner * feats + main, EXTRA)
         for i in range(3):
+            if i > 0:
+                block = y_block(i, j)
+                remote(block, block, y_send.at[j, i], y_recv.at[j, i], y_bwd).wait_recv()
             grad += times(ry[i, rows, :], owners[i] * feats, main)
 
-        meta = ro[rows, width - META : width].astype(F32)
+        meta = ro[rows, feats : feats + META].astype(F32)
         lanes = lax.broadcasted_iota(jnp.int32, (ROWS, META), 1)
         weight = (
             pltpu.roll(meta, META - 8, 1) + pltpu.roll(meta, META - 16, 1)
@@ -278,8 +324,10 @@
         sl[y, pl.ds(zz, 1), 0:ROWS] = jnp.sum(part.T, axis=0, keepdims=True)
         scaled = prob * grad
         slope = sigmoid * (1.0 + gate * (1.0 - sigmoid))
-        gg_ref[place, :] = (scaled * up * slope).astype(BF16)
-        gu_ref[place, :] = (scaled * activation).astype(BF16)
+        gg[place, :] = (scaled * up * slope).astype(BF16)
+        gu[place, :] = (scaled * activation).astype(BF16)
+        store(gg.at[place], gg_hbm.at[place], o_sem.at[j, 0])
+        store(gu.at[place], gu_hbm.at[place], o_sem.at[j, 1])
 
     stage = {"T": take_tokens, "P": pack, "Y": send_y, "R": y_relay, "C": compute}
     for name in ORDER.split():
@@ -296,7 +344,9 @@
     def weights(block, at, size):
         for piece, wide in chunks(size, 256):
             total = jnp.dot(hst[...], block(piece, wide), preferred_element_type=F32)
-            gw_ref[:, columns(at + piece, wide)] = total.astype(BF16)
+            gw[:, columns(at + piece, wide)] = total.astype(BF16)
+        done = columns(at, size)
+        store(gw.at[:, done], gw_hbm.at[:, done], w_sem.at[len(stores) - 2 * NZ])
 
     weights(lambda at, size: ro[:, at : at + size], y * feats, feats)
 
@@ -308,7 +358,7 @@
 
     for s in range(3):
         owner = (y + 1 + s) % 4
-        base = feats + s * EXTRA
+        base = extras + s * EXTRA
         weights(lambda at, size: ro[:, base + at : base + at + size], owner * feats + main, EXTRA)
 
     for i, away in enumerate((-d, 2, d)):
@@ -357,8 +407,35 @@
         back_ref[k : k + 1, :] = jnp.sum(
             jnp.where(slots == wanted[k : k + 1], total, 0.0), axis=0, keepdims=True
         )
+    for copy in stores:
+        copy.wait()
     for copy in sends:
         copy.wait_send()
+
+
+def hand_over(*refs):
+    arrays = 3
+    inputs, small_in, outputs, small_out = refs[0:3], refs[3], refs[4:7], refs[7]
+    held, sem = refs[8:11], refs[11]
+    loads, stores = [], []
+    for i in range(arrays):
+        size = inputs[i].shape[0] // PARTS
+        for part in range(PARTS):
+            rows = pl.ds(part * size, size)
+            loads.append(
+                pltpu.make_async_copy(inputs[i].at[rows], held[i].at[rows], sem.at[0, i, part])
+            )
+            stores.append(
+                pltpu.make_async_copy(held[i].at[rows], outputs[i].at[rows], sem.at[1, i, part])
+            )
+    for load in loads:
+        load.start()
+    small_out[...] = small_in[...]
+    for load, store in zip(loads, stores):
+        load.wait()
+        store.start()
+    for store in stores:
+        store.wait()
 
 
 def body(grad_out, routes, gates, saved_gate, saved_up, w_down):
@@ -382,7 +459,7 @@
             jax.ShapeDtypeStruct((TOP, TOK), F32),
         ),
         in_specs=[vmem, vmem, vmem, hbm, hbm, hbm],
-        out_specs=(vmem, vmem, vmem, vmem),
+        out_specs=(hbm, hbm, hbm, vmem),
         scratch_shapes=[
             pltpu.VMEM((NZ, 2 * TOK, width), BF16),
             pltpu.VMEM((NZ, 3 * SLAB, width), BF16),
@@ -393,6 +470,9 @@
             pltpu.VMEM((slots, hidden_units), BF16),
             pltpu.VMEM((slots, hidden_units), BF16),
             pltpu.VMEM((hidden_units, slots), BF16),
+            pltpu.VMEM((slots, hidden_units), BF16),
+            pltpu.VMEM((slots, hidden_units), BF16),
+            pltpu.VMEM((hidden_units, feats * NY), BF16),
             pltpu.VMEM((META, TOK), F32),
             pltpu.VMEM((NY, NZ, 256), F32),
             pltpu.VMEM((NX, NZ, 256), F32),
@@ -400,14 +480,16 @@
             pltpu.VMEM((NZ, 8, 128), F32),
             pltpu.VMEM((NZ, 8, 128), F32),
             dma((3,)),
-            dma((3,)),
-            dma((3,)),
+            dma((NZ, 2)),
+            dma((7,)),
+            dma((5,)),
+            dma((5,)),
             dma((NZ,)),
             dma((NZ,)),
-            dma((NZ,)),
-            dma((NZ,)),
-            dma((NZ, 3)),
-            dma((NZ, 3)),
+            dma((NZ + 1,)),
+            dma((NZ + 1,)),
+            dma((NZ, 6)),
+            dma((NZ, 6)),
             dma((NZ, 3)),
             dma((NZ, 3)),
             dma((7,)),
@@ -430,6 +512,14 @@
         w_down[0],
     )
 
+    results = (grad_gate, grad_up, grad_w, back)
+    grad_gate, grad_up, grad_w, back = pl.pallas_call(
+        hand_over,
+        out_shape=tuple(jax.ShapeDtypeStruct(a.shape, a.dtype) for a in results),
+        in_specs=[hbm, hbm, hbm, vmem],
+        out_specs=(hbm, hbm, hbm, vmem),
+        scratch_shapes=[pltpu.VMEM(a.shape, a.dtype) for a in results[0:3]] + [dma((2, 3, PARTS))],
+    )(*results)
     return (
         grad_gate.reshape(saved_gate.shape),
         grad_up.reshape(saved_up.shape),

time: 160 us -> 141 us (0.88)
  Pallas kernels: 151 us -> 141 us
  local copies, waits for them, and re-layouts: 7.48 us -> 0 us
    pallas_call x1, Pallas kernels: 151 us -> 134 us  [body(): pl.pallas_call(functools.partial(kernel, feats, width), out_shape=(jax.Sh...]
    unnamed x8 -> x0, local copies, waits for them, and re-layouts: 7.48 us -> none
    pallas_call x0 -> x1, Pallas kernels: none -> 6.53 us  [body(): pl.pallas_call(hand_over, out_shape=tuple((jax.ShapeDtypeStruct(a.shape,...]
where the time goes in v3:
time: 141 us
  Pallas kernels  141 us (100%)
    pallas_call x1, Pallas kernels, body(): pl.pallas_call(functools.partial(kernel, feats, width), out_shape=(jax.Sh...  134 us
    pallas_call x1, Pallas kernels, body(): pl.pallas_call(hand_over, out_shape=tuple((jax.ShapeDtypeStruct(a.shape,...  6.53 us

profile of v3, /device:TPU:1, one launch (start us, length us, event | category | flops | bytes accessed | tf_op | source)
XLA Modules:
  0.0 141.3 jit_solution(262848021870778263)
XLA Ops:
  0.6 134.0 %shard_map.93 = (bf16[1536,384]{1,0:T(8,128)(2,1)}, bf16[1536,384]{1,0:T(8,128)(2,1)}, bf16[384,5120]{1,0:T(8,128)(2,1)}, f32[6,128]{1,0:T(8,128)}) custom-call(bf16[128,1280]{1,0:T(8,128)(2,1)} %tok_ref.1, s32[6,128]{1,0:T(8,128)} %bitcast.15, f32[6,128]{1,0:T(8,128)} %bitcast.16, bf16[1536,384]{1,0:T(8,128)(2,1)} %bitcast.11, bf16[1536,384]{1,0:T(8,128)(2,1)} %bitcast.12, ...), custom_call_target="tpu_custom_call" | custom-call | flops 12079595520 | bytes 16777216 | tf_op jit(solution)/shard_map/pallas_call | solution.py:453
  134.6 6.5 %shard_map.94 = (bf16[1536,384]{1,0:T(8,128)(2,1)}, bf16[1536,384]{1,0:T(8,128)(2,1)}, bf16[384,5120]{1,0:T(8,128)(2,1)}, f32[6,128]{1,0:T(8,128)}) custom-call(bf16[1536,384]{1,0:T(8,128)(2,1)} %get-tuple-element.12.refs_0_, bf16[1536,384]{1,0:T(8,128)(2,1)} %get-tuple-element.13.refs_1_, bf16[384,5120]{1,0:T(8,128)(2,1)} %get-tuple-element.14.refs_2_, ...), custom_call_target="tpu_custom_call" | custom-call | tf_op jit(solution)/shard_map/pallas_call | solution.py:516

commit v4 on v3

--- a/solution.py
+++ b/solution.py
@@ -41,9 +41,9 @@
     gate_hbm,
     up_hbm,
     w_hbm,
-    gg_hbm,
-    gu_hbm,
-    gw_hbm,
+    gg,
+    gu,
+    gw,
     back_ref,
     tok,
     pk,
@@ -54,18 +54,12 @@
     su,
     hs,
     hst,
-    gg,
-    gu,
-    gw,
     table,
     sl,
     sums,
-    theirs,
     zs,
     zr,
     in_sem,
-    o_sem,
-    w_sem,
     e_send,
     e_recv,
     z_send,
@@ -102,7 +96,9 @@
 
     barrier = pltpu.get_barrier_semaphore()
     z_far = [ep_at((z + o) % 8, x, c) for o in range(2, 7)]
-    for peer in [z_fwd, z_bwd, x_fwd, x_far, x_bwd, y_fwd, y_far, y_bwd, partner] + z_far:
+    x_other = [ep_at(z, (x + o) % 4, 1 - c) for o in range(1, NX)]
+    peers = [z_fwd, z_bwd, x_fwd, x_far, x_bwd, y_fwd, y_far, y_bwd, partner]
+    for peer in peers + z_far + x_other:
         pl.semaphore_signal(barrier, inc=1, device_id=peer, device_id_type=MESH)
 
     loads = [
@@ -139,7 +135,7 @@
         )
     tok[0, 0:TOK, feats : feats + META] = table[...].T.astype(BF16)
     sl[...] = jnp.zeros(sl.shape, F32)
-    pl.semaphore_wait(barrier, 14)
+    pl.semaphore_wait(barrier, 17)
 
     sends = []
 
@@ -267,13 +263,6 @@
         remote(y_block(0, j), y_block(0, j), y_send.at[j, 0], y_recv.at[j, 0], y_bwd).wait_recv()
         start(y_block(0, j), y_block(2, j), y_send.at[j, 2], y_recv.at[j, 2], y_fwd)
 
-    stores = []
-
-    def store(src, dst, sem):
-        copy = pltpu.make_async_copy(src, dst, sem)
-        copy.start()
-        stores.append(copy)
-
     def columns(at, size):
         return pl.ds(pl.multiple_of(at, 128), size)
 
@@ -326,8 +315,6 @@
         slope = sigmoid * (1.0 + gate * (1.0 - sigmoid))
         gg[place, :] = (scaled * up * slope).astype(BF16)
         gu[place, :] = (scaled * activation).astype(BF16)
-        store(gg.at[place], gg_hbm.at[place], o_sem.at[j, 0])
-        store(gu.at[place], gu_hbm.at[place], o_sem.at[j, 1])
 
     stage = {"T": take_tokens, "P": pack, "Y": send_y, "R": y_relay, "C": compute}
     for name in ORDER.split():
@@ -345,34 +332,27 @@
         for piece, wide in chunks(size, 256):
             total = jnp.dot(hst[...], block(piece, wide), preferred_element_type=F32)
             gw[:, columns(at + piece, wide)] = total.astype(BF16)
-        done = columns(at, size)
-        store(gw.at[:, done], gw_hbm.at[:, done], w_sem.at[len(stores) - 2 * NZ])
 
     weights(lambda at, size: ro[:, at : at + size], y * feats, feats)
 
     for i, away in enumerate((-d, 2, d)):
         wait(sl.at[(y + away + 4) % 4], s_recv.at[i])
-    sums[x] = ((sl[0] + sl[1]) + sl[2]) + sl[3]
-    for i, peer in enumerate((x_fwd, x_far, x_bwd)):
-        start(sums.at[x], sums.at[x], s_send.at[3 + i], s_recv.at[3 + i], peer)
+    me = 2 * x + c
+    sums[me] = ((sl[0] + sl[1]) + sl[2]) + sl[3]
+    for o in range(1, 2 * NX):
+        peer = ep_at(z, (x + o // 2) % 4, (c + o) % 2)
+        start(sums.at[me], sums.at[me], s_send.at[2 + o], s_recv.at[2 + o], peer)
 
     for s in range(3):
         owner = (y + 1 + s) % 4
         base = extras + s * EXTRA
         weights(lambda at, size: ro[:, base + at : base + at + size], owner * feats + main, EXTRA)
 
-    for i, away in enumerate((-d, 2, d)):
-        wait(sums.at[(x + away + 4) % 4], s_recv.at[3 + i])
-    start(sums, theirs, s_send.at[6], s_recv.at[6], partner)
-
-    weights(lambda at, size: ry[0, :, at : at + size], owners[0] * feats, main)
-
-    wait(theirs, s_recv.at[6])
+    for o in range(1, 2 * NX):
+        wait(sums.at[2 * ((x - o // 2 + 4) % 4) + (c + o) % 2], s_recv.at[2 + o])
     shift = (256 - (x * SLAB + c * CAP)) % 256
-    for i in range(NX):
-        for core in range(2):
-            block = jnp.where(c == core, sums[i], theirs[i])
-            zs[:, 2 * i + core, :] = pltpu.roll(block, shift, 1)[:, 0:128]
+    for i in range(2 * NX):
+        zs[:, i, :] = pltpu.roll(sums[i], shift, 1)[:, 0:128]
     for o in range(1, NZ):
         start(
             zs.at[(z + o) % 8],
@@ -383,7 +363,7 @@
         )
     zr[z] = zs[z]
 
-    for i in range(1, 3):
+    for i in range(3):
         weights(lambda at, size: ry[i, :, at : at + size], owners[i] * feats, main)
 
     for o in range(1, NZ):
@@ -407,35 +387,25 @@
         back_ref[k : k + 1, :] = jnp.sum(
             jnp.where(slots == wanted[k : k + 1], total, 0.0), axis=0, keepdims=True
         )
-    for copy in stores:
-        copy.wait()
     for copy in sends:
         copy.wait_send()
 
 
 def hand_over(*refs):
-    arrays = 3
-    inputs, small_in, outputs, small_out = refs[0:3], refs[3], refs[4:7], refs[7]
-    held, sem = refs[8:11], refs[11]
-    loads, stores = [], []
-    for i in range(arrays):
+    inputs, small_in, outputs, small_out, sem = refs[0:3], refs[3], refs[4:7], refs[7], refs[8]
+    copies = []
+    for i in range(3):
         size = inputs[i].shape[0] // PARTS
         for part in range(PARTS):
             rows = pl.ds(part * size, size)
-            loads.append(
-                pltpu.make_async_copy(inputs[i].at[rows], held[i].at[rows], sem.at[0, i, part])
+            copies.append(
+                pltpu.make_async_copy(inputs[i].at[rows], outputs[i].at[rows], sem.at[i, part])
             )
-            stores.append(
-                pltpu.make_async_copy(held[i].at[rows], outputs[i].at[rows], sem.at[1, i, part])
-            )
-    for load in loads:
-        load.start()
+    for copy in copies:
+        copy.start()
     small_out[...] = small_in[...]
-    for load, store in zip(loads, stores):
-        load.wait()
-        store.start()
-    for store in stores:
-        store.wait()
+    for copy in copies:
+        copy.wait()
 
 
 def body(grad_out, routes, gates, saved_gate, saved_up, w_down):
@@ -453,13 +423,13 @@
     grad_gate, grad_up, grad_w, back = pl.pallas_call(
         functools.partial(kernel, feats, width),
         out_shape=(
-            jax.ShapeDtypeStruct((slots, hidden_units), BF16),
-            jax.ShapeDtypeStruct((slots, hidden_units), BF16),
-            jax.ShapeDtypeStruct((hidden_units, feats * NY), BF16),
+            pltpu.VMEM((slots, hidden_units), BF16),
+            pltpu.VMEM((slots, hidden_units), BF16),
+            pltpu.VMEM((hidden_units, feats * NY), BF16),
             jax.ShapeDtypeStruct((TOP, TOK), F32),
         ),
         in_specs=[vmem, vmem, vmem, hbm, hbm, hbm],
-        out_specs=(hbm, hbm, hbm, vmem),
+        out_specs=(vmem, vmem, vmem, vmem),
         scratch_shapes=[
             pltpu.VMEM((NZ, 2 * TOK, width), BF16),
             pltpu.VMEM((NZ, 3 * SLAB, width), BF16),
@@ -470,18 +440,12 @@
             pltpu.VMEM((slots, hidden_units), BF16),
             pltpu.VMEM((slots, hidden_units), BF16),
             pltpu.VMEM((hidden_units, slots), BF16),
-            pltpu.VMEM((slots, hidden_units), BF16),
-            pltpu.VMEM((slots, hidden_units), BF16),
-            pltpu.VMEM((hidden_units, feats * NY), BF16),
             pltpu.VMEM((META, TOK), F32),
             pltpu.VMEM((NY, NZ, 256), F32),
-            pltpu.VMEM((NX, NZ, 256), F32),
-            pltpu.VMEM((NX, NZ, 256), F32),
+            pltpu.VMEM((2 * NX, NZ, 256), F32),
             pltpu.VMEM((NZ, 8, 128), F32),
             pltpu.VMEM((NZ, 8, 128), F32),
             dma((3,)),
-            dma((NZ, 2)),
-            dma((7,)),
             dma((5,)),
             dma((5,)),
             dma((NZ,)),
@@ -492,13 +456,13 @@
             dma((NZ, 6)),
             dma((NZ, 3)),
             dma((NZ, 3)),
-            dma((7,)),
-            dma((7,)),
+            dma((2 + 2 * NX,)),
+            dma((2 + 2 * NX,)),
             dma((NZ,)),
             dma((NZ,)),
         ],
         compiler_params=pltpu.CompilerParams(
-            collective_id=0, has_side_effects=True, vmem_limit_bytes=60 * 1024 * 1024
+            collective_id=0, has_side_effects=True, vmem_limit_bytes=52 * 1024 * 1024
         ),
         cost_estimate=pl.CostEstimate(
             flops=flops, bytes_accessed=16 * 1024 * 1024, transcendentals=slots * hidden_units
@@ -516,9 +480,10 @@
     grad_gate, grad_up, grad_w, back = pl.pallas_call(
         hand_over,
         out_shape=tuple(jax.ShapeDtypeStruct(a.shape, a.dtype) for a in results),
-        in_specs=[hbm, hbm, hbm, vmem],
+        in_specs=[vmem, vmem, vmem, vmem],
         out_specs=(hbm, hbm, hbm, vmem),
-        scratch_shapes=[pltpu.VMEM(a.shape, a.dtype) for a in results[0:3]] + [dma((2, 3, PARTS))],
+        scratch_shapes=[dma((3, PARTS))],
+        compiler_params=pltpu.CompilerParams(vmem_limit_bytes=16 * 1024 * 1024),
     )(*results)
     return (
         grad_gate.reshape(saved_gate.shape),

time: 141 us -> 139 us (0.986)
  Pallas kernels: 141 us -> 138 us
    pallas_call x1, Pallas kernels: 6.53 us -> 3.36 us  [body(): pl.pallas_call(hand_over, out_shape=tuple((jax.ShapeDtypeStruct(a.shape,...]
where the time goes in v4:
time: 139 us
  Pallas kernels  138 us (99%)
    pallas_call x1, Pallas kernels, body(): pl.pallas_call(functools.partial(kernel, feats, width), out_shape=(pltpu....  134 us
    pallas_call x1, Pallas kernels, body(): pl.pallas_call(hand_over, out_shape=tuple((jax.ShapeDtypeStruct(a.shape,...  3.36 us

profile of v4, /device:TPU:1, one launch (start us, length us, event | category | flops | bytes accessed | tf_op | source)
XLA Modules:
  0.0 139.1 jit_solution(371524413233293809)
XLA Ops:
  0.6 134.2 %shard_map.93 = (bf16[1536,384]{1,0:T(8,128)(2,1)S(1)}, bf16[1536,384]{1,0:T(8,128)(2,1)S(1)}, bf16[384,5120]{1,0:T(8,128)(2,1)S(1)}, f32[6,128]{1,0:T(8,128)}) custom-call(bf16[128,1280]{1,0:T(8,128)(2,1)} %tok_ref.1, s32[6,128]{1,0:T(8,128)} %bitcast.15, f32[6,128]{1,0:T(8,128)} %bitcast.16, bf16[1536,384]{1,0:T(8,128)(2,1)} %bitcast.11, ...), custom_call_target="tpu_custom_call" | custom-call | flops 12079595520 | bytes 16777216 | tf_op jit(solution)/shard_map/pallas_call | solution.py:423
  134.9 0.0 copy-start
  134.9 0.7 copy-done
  135.5 3.4 %shard_map.94 = (bf16[1536,384]{1,0:T(8,128)(2,1)}, bf16[1536,384]{1,0:T(8,128)(2,1)}, bf16[384,5120]{1,0:T(8,128)(2,1)}, f32[6,128]{1,0:T(8,128)}) custom-call(bf16[1536,384]{1,0:T(8,128)(2,1)S(1)} %get-tuple-element.12.refs_0_, bf16[1536,384]{1,0:T(8,128)(2,1)S(1)} %get-tuple-element.13.refs_1_, bf16[384,5120]{1,0:T(8,128)(2,1)S(1)} %get-tuple-element.14.refs_2_, ...), custom_call_target="tpu_custom_call" | custom-call | tf_op jit(solution)/shard_map/pallas_call | solution.py:480
Async XLA Ops:
  134.9 0.7 copy-start
